TPU v7x, 32 devices: a whole 2x2x4 slice. The times are simulated.
32 devices in a mesh: depth: 8 (over z, core), coef: 4 (over y, x).
Axes of the slice: x: 2, y: 2, z: 4, core: 2. Of those that a mesh axis runs over, the one named last changes fastest.
Arguments:
- volume: bfloat16 [32, 64, 64, 512], P('depth', None, 'coef'), may hold values from -1 to 1
- shift: int32 [32], P('depth'), may hold values from -64 to 64
- frac: int32 [32], P('depth'), may hold values from 0 to 16
- basis: bfloat16 [64, 64], replicated, may hold values from -0.75 to 0.75
- data: float32 [64, 64, 512], P(('depth', 'coef')), may hold values from 0.05 to 4
- mask: int32 [64, 64, 512], P(('depth', 'coef')), may hold values 0 or 1
Outputs:
- gradient: bfloat16 [32, 64, 64, 512], P('depth', None, 'coef')
- residual: bfloat16 [64, 64, 512], P(('depth', 'coef'))
All inputs are finite; a program needn't handle non-finite values. No bound on the sum of `mask` on one device may be relied on, other than what follows from the above.
Results may differ from a plain program's by a relative error of at most 0.0053.
Values may be sent and summed in bfloat16 or wider, within the bound.
No kernel may reach another device: no remote copies, remote signals or barrier semaphores. Data moves between devices by JAX's collectives and lax.ppermute only.
A program may use at most 128 MiB of HBM per device.

v0:
```python
import functools

import jax
import jax.numpy as jnp
from jax import lax
from jax.experimental import pallas as pl
from jax.experimental.pallas import tpu as pltpu
from jax.sharding import PartitionSpec as P

F32, BF16 = jnp.float32, jnp.bfloat16
MIB = 1024 * 1024
NEAR = 2
PARAMS = pltpu.CompilerParams(vmem_limit_bytes=44 * MIB)
WIDE = pltpu.CompilerParams(vmem_limit_bytes=50 * MIB)


def weigh(steps, number):
    weight = (number & 31).astype(F32) / 16.0
    offset = steps - lax.shift_right_arithmetic(number, 5)
    return jnp.where(offset == 0, 1.0 - weight, jnp.where(offset == 1, weight, 0.0)).astype(BF16)


def window(side, half):
    return (0, half + half // 2) if side == 0 else (half // 2, 2 * half)


def fill_forward(tables, offsets):
    _, layers, span, half = tables.shape
    for side in range(2):
        low, _ = window(side, half)
        row = lax.broadcasted_iota(jnp.int32, (span, half), 0) + low
        column = lax.broadcasted_iota(jnp.int32, (span, half), 1) + side * half
        for layer in range(layers):
            tables[side, layer] = weigh(column - row, offsets[layer])


def fill_back(tables, offsets):
    _, layers, half, _ = tables.shape
    quarter = half // 2
    row = lax.broadcasted_iota(jnp.int32, (half, half), 0)
    column = lax.broadcasted_iota(jnp.int32, (half, half), 1)
    for layer in range(layers):
        weights = weigh(row - column, offsets[layer])
        none = jnp.zeros((quarter, quarter), BF16)
        tables[0, layer] = weights
        tables[1, layer, :quarter, :quarter] = none
        tables[1, layer, quarter:, quarter:] = none
        tables[1, layer, :quarter, quarter:] = weights[:quarter, quarter:]
        tables[1, layer, quarter:, :quarter] = weights[quarter:, :quarter]


def interpolate(block, diagonal, corner):
    rows, width = block.shape
    half, quarter = width // 2, width // 4
    halves = jnp.concatenate([block[:, :half], block[:, half:]], axis=0)
    main = jnp.dot(halves, diagonal, preferred_element_type=F32)
    cross = jnp.dot(block[:, quarter : quarter + half], corner, preferred_element_type=F32)
    left, right = main[:rows], main[rows:]
    pieces = [
        left[:, :quarter],
        left[:, quarter:] + cross[:, :quarter],
        right[:, :quarter] + cross[:, quarter:],
        right[:, quarter:],
    ]
    return jnp.concatenate(pieces, axis=1)


def turns(chips):
    return [f * NEAR + n for n in range(NEAR) for f in reversed(range(chips // NEAR))]


def project_kernel(own, numbers, volume, out, *refs):
    offsets, small, tables, slab, sems = refs[-5:]
    layers, chips, _, m, width = volume.shape
    half = width // 2
    order = turns(chips)
    core = lax.axis_index("core")
    which = core if own else 1 - core

    def fetch(layer, step):
        return pltpu.make_async_copy(
            volume.at[layer, order[step], which], slab.at[layer, step], sems.at[layer, step]
        )

    brought = pltpu.make_async_copy(numbers, offsets, small)
    brought.start()
    for layer in range(layers):
        for step in range(chips):
            fetch(layer, step).start()
    brought.wait()
    fill_forward(tables, offsets)
    if own:
        fill_back(refs[0], offsets)
    for layer in range(layers):
        for step in range(chips):
            fetch(layer, step).wait()
    for side in range(2):
        low, high = window(side, half)
        rows = [slab[layer].reshape(chips * m, width)[:, low:high] for layer in range(layers)]
        total = jnp.dot(
            jnp.concatenate(rows, axis=1),
            tables[side].reshape(layers * (high - low), half),
            preferred_element_type=F32,
        ).astype(out.dtype)
        out[:, :, side * half : (side + 1) * half] = total.reshape(chips, m, half)


def misfit_kernel(chips, basis, data, mask, sums_of, residual, back):
    slots, part, width = back.shape
    coef = slots // chips
    rows, segments, _ = data.shape
    local_k = part // rows
    sums = []
    for c in range(coef):
        total = sums_of[c * chips].astype(F32)
        for step in range(1, chips):
            total = total + sums_of[c * chips + step].astype(F32)
        sums.append(total)
    pixels = [
        jnp.concatenate([s[r * local_k : (r + 1) * local_k] for s in sums], axis=0)
        for r in range(rows)
    ]
    pixels = jnp.concatenate(pixels, axis=1)
    top = pixels.astype(BF16)
    rest = pixels - top.astype(F32)
    middle = rest.astype(BF16)
    bottom = (rest - middle.astype(F32)).astype(BF16)
    predicted = lax.dot_general(
        jnp.concatenate([basis[...]] * 3, axis=0),
        jnp.concatenate([top, middle, bottom], axis=0),
        (((0,), (0,)), ((), ())),
        preferred_element_type=F32,
    )
    left = [
        mask[r].astype(F32) * (predicted[:, r * width : (r + 1) * width] - jnp.sqrt(data[r]))
        for r in range(rows)
    ]
    left = [x.astype(BF16) for x in left]
    for r in range(rows):
        residual[r] = left[r]
    backs = 2.0 * jnp.dot(basis[...], jnp.concatenate(left, axis=1), preferred_element_type=F32)
    for c in range(coef):
        piece = backs[c * local_k : (c + 1) * local_k]
        piece = [piece[:, r * width : (r + 1) * width] for r in range(rows)]
        piece = jnp.concatenate(piece, axis=0).astype(BF16)
        for step in range(chips):
            back[c * chips + step] = piece


def spread_kernel(own, tables, grad, *refs):
    out, staged, sems = refs[-3:]
    layers, chips, _, m, width = out.shape
    core = lax.axis_index("core")
    which = core if own else 1 - core

    def store(layer, step):
        return pltpu.make_async_copy(
            staged.at[layer, step], out.at[layer, order[step], which], sems.at[layer, step]
        )

    coef = grad.shape[0] // chips
    order = turns(chips)
    joined = [grad[c * chips + step] for step in range(chips) for c in range(coef)]
    joined = jnp.concatenate(joined, axis=0)
    for layer in range(layers):
        slab = interpolate(joined, tables[0, layer], tables[1, layer])
        staged[layer] = slab.reshape(chips, m, width).astype(BF16)
        for step in range(chips):
            store(layer, step).start()
    for layer in range(layers):
        for step in range(chips):
            store(layer, step).wait()


def shards(volume, shift, frac, basis, data, mask):
    layers, height, local_k, width = volume.shape
    chips, coef = lax.axis_size("chip"), lax.axis_size("coef")
    rows = height // (2 * chips * coef)
    half = width // 2
    part = rows * local_k
    m = coef * part
    vmem = pl.BlockSpec(memory_space=pltpu.VMEM)
    hbm = pl.BlockSpec(memory_space=pltpu.HBM)

    def shape(*dims, dtype=BF16):
        return jax.ShapeDtypeStruct(dims, dtype)

    slots = (chips * coef, part, width)
    weights = shape(2, layers, half, half)

    def swap(x):
        return lax.ppermute(x, "core", [(0, 1), (1, 0)])

    groups = [
        [(chip * 2 + core) * coef + c for c in range(coef) for chip in turns(chips)]
        for core in range(2)
    ]

    def exchange(x):
        axes = ("chip", "core", "coef")
        return lax.all_to_all(
            x, axes, split_axis=0, concat_axis=0, tiled=True, axis_index_groups=groups
        )

    offsets = shift * 32 + frac
    parts = volume.reshape(layers, chips, 2, m, width)

    def project(own):
        sums = shape(chips, m, width, dtype=F32 if own else BF16)
        return pl.pallas_call(
            functools.partial(project_kernel, own),
            out_shape=[sums, weights] if own else sums,
            in_specs=[hbm, hbm],
            out_specs=[vmem, vmem] if own else vmem,
            scratch_shapes=[
                pltpu.SMEM((layers,), jnp.int32),
                pltpu.SemaphoreType.DMA,
                pltpu.VMEM((2, layers, half + half // 2, half), BF16),
                pltpu.VMEM((layers, chips, m, width), BF16),
                pltpu.SemaphoreType.DMA((layers, chips)),
            ],
            compiler_params=WIDE,
            name="project" + ("_own" if own else ""),
        )(offsets, parts)

    theirs = swap(project(False))
    mine, tables = project(True)
    sums = (mine + theirs.astype(F32)).astype(BF16)
    sums = sums.reshape(chips, coef, part, width).transpose(1, 0, 2, 3)
    sums = exchange(sums.reshape(slots))
    residual, back = pl.pallas_call(
        functools.partial(misfit_kernel, chips),
        out_shape=[shape(*data.shape), shape(*slots)],
        in_specs=[vmem] * 4,
        out_specs=[vmem] * 2,
        compiler_params=PARAMS,
        name="misfit",
    )(basis, data, mask, sums)
    grad = exchange(back)

    def spread(grad, partial=None):
        own = partial is None
        return pl.pallas_call(
            functools.partial(spread_kernel, own),
            out_shape=shape(layers, chips, 2, m, width),
            in_specs=[vmem, vmem] + [hbm] * (not own),
            out_specs=hbm,
            scratch_shapes=[
                pltpu.VMEM((layers, chips, m, width), BF16),
                pltpu.SemaphoreType.DMA((layers, chips)),
            ],
            input_output_aliases={} if own else {2: 0},
            compiler_params=PARAMS,
            name="spread" + ("_own" if own else ""),
        )(tables, grad, *([] if own else [partial]))

    gradient = spread(swap(grad), spread(grad))
    return gradient.reshape(volume.shape), residual


def solution(mesh):
    depth, coef = mesh.shape["depth"], mesh.shape["coef"]
    devices = mesh.devices.reshape(depth // 2, 2, coef)
    mesh = jax.sharding.Mesh(devices, ("chip", "core", "coef"))
    deep = ("chip", "core")
    cube = P(deep, None, "coef", None)
    pixel = P(deep + ("coef",), None, None)
    in_specs = (cube, P(deep), P(deep), P(), pixel, pixel)
    out_specs = (cube, pixel)
    return jax.shard_map(shards, mesh=mesh, in_specs=in_specs, out_specs=out_specs, check_vma=False)
```

profile of v0, /device:TPU:1, one launch (start us, length us, event | category | flops | bytes accessed | tf_op | source)
XLA Modules:
  0.0 51.4 jit_solution(8693667453097752138)
XLA Ops:
  0.6 0.7 %multiply_add_fusion.numbers = s32[4]{0:T(128)S(1)} fusion(s32[4]{0:T(128)} %param.8, s32[4]{0:T(128)} %param.7), kind=kLoop, calls=%fused_computation.1 | loop fusion | flops 8 | bytes 48 | tf_op jit(solution)/shard_map/add | solution.py:205
  1.3 2.7 %project.1 = bf16[4,128,512]{2,1,0:T(8,128)(2,1)S(1)} custom-call(s32[4]{0:T(128)S(1)} %multiply_add_fusion.numbers, bf16[4,4,2,128,512]{4,3,2,1,0:T(8,128)(2,1)} %bitcast.6), custom_call_target="tpu_custom_call" | custom-call | tf_op jit(solution)/shard_map/project/pallas_call | solution.py:210
  4.0 0.0 copy-start
  4.0 0.0 copy-start.1
  4.1 0.0 copy-start.2
  4.1 0.1 collective-permute-start
  4.2 2.7 %project_own.1 = (f32[4,128,512]{2,1,0:T(8,128)S(1)}, bf16[2,4,256,256]{3,2,1,0:T(8,128)(2,1)S(1)}) custom-call(s32[4]{0:T(128)S(1)} %multiply_add_fusion.numbers, bf16[4,4,2,128,512]{4,3,2,1,0:T(8,128)(2,1)} %bitcast.7), custom_call_target="tpu_custom_call" | custom-call | tf_op jit(solution)/shard_map/project_own/pallas_call | solution.py:210
  6.9 0.0 collective-permute-done
  7.0 0.2 add_convert_fusion
  7.2 20.4 %all_to_all.10.sums_of = bf16[16,32,512]{2,1,0:T(8,128)(2,1)S(1)} all-to-all(bf16[16,32,512]{2,1,0:T(8,128)(2,1)S(1)} %bitcast.9), channel_id=1, replica_groups={{16,0,24,8,17,1,25,9,18,2,26,10,19,3,27,11},{20,4,28,12,21,5,29,13,22,6..., dimensions={0} | all-to-all | bytes 1048576 | tf_op jit(solution)/shard_map/all_to_all | solution.py:201
  27.6 0.0 copy-done
  27.6 0.0 copy-done.1
  27.6 0.0 copy-done.2
  27.6 0.9 %misfit.1 = (bf16[2,64,512]{2,1,0:T(8,128)(2,1)}, bf16[16,32,512]{2,1,0:T(8,128)(2,1)S(1)}) custom-call(bf16[64,64]{1,0:T(8,128)(2,1)S(1)} %copy-done.2, f32[2,64,512]{2,1,0:T(8,128)S(1)} %copy-done, s32[2,64,512]{2,1,0:T(8,128)S(1)} %copy-done.1, bf16[16,32,512]{2,1,0:T(8,128)(2,1)S(1)} %all_to_all.10.sums_of), custom_call_target="tpu_custom_call" | custom-call | tf_op jit(solution)/shard_map/misfit/pallas_call | solution.py:231
  28.5 13.1 %all_to_all.11.grad = bf16[16,32,512]{2,1,0:T(8,128)(2,1)S(1)} all-to-all(bf16[16,32,512]{2,1,0:T(8,128)(2,1)S(1)} %get-tuple-element.8), channel_id=1, replica_groups={{16,0,24,8,17,1,25,9,18,2,26,10,19,3,27,11},{20,4,28,12,21,5,29,13,22,6..., dimensions={0} | all-to-all | bytes 1048576 | tf_op jit(solution)/shard_map/all_to_all | solution.py:201
  41.6 5.8 %collective-permute-start.1 = (bf16[16,32,512]{2,1,0:T(8,128)(2,1)S(1)}, bf16[16,32,512]{2,1,0:T(8,128)(2,1)S(1)}, u32[]{:S(2)}, u32[]{:S(2)}) collective-permute-start(bf16[16,32,512]{2,1,0:T(8,128)(2,1)S(1)} %all_to_all.11.grad), channel_id=1, source_target_pairs={{0,4},{4,0},{1,5},{5,1},{2,6},{6,2},{3,7},{7,3},{8,12},{12,8},{9,1... | collective-permute-start | bytes 1572872 | tf_op jit(solution)/shard_map/ppermute | solution.py:192
  47.5 1.9 %spread_own.1.refs_0_ = bf16[4,4,2,128,512]{4,3,2,1,0:T(8,128)(2,1)} custom-call(bf16[2,4,256,256]{3,2,1,0:T(8,128)(2,1)S(1)} %get-tuple-element.6.tables, bf16[16,32,512]{2,1,0:T(8,128)(2,1)S(1)} %all_to_all.11.grad), custom_call_target="tpu_custom_call" | custom-call | tf_op jit(solution)/shard_map/spread_own/pallas_call | solution.py:243
  49.4 0.0 collective-permute-done.1.grad
  49.4 2.0 %spread.1 = bf16[4,4,2,128,512]{4,3,2,1,0:T(8,128)(2,1)} custom-call(bf16[2,4,256,256]{3,2,1,0:T(8,128)(2,1)S(1)} %get-tuple-element.6.tables, bf16[16,32,512]{2,1,0:T(8,128)(2,1)S(1)} %collective-permute-done.1.grad, bf16[4,4,2,128,512]{4,3,2,1,0:T(8,128)(2,1)} %spread_own.1.refs_0_), custom_call_target="tpu_custom_call", output_to_operand_aliasing={{}: (2, {})} | custom-call | tf_op jit(solution)/shard_map/spread/pallas_call | solution.py:243
  (1 shorter events, 0.0 us)
Async XLA Ops:
  4.0 23.5 %copy-start = (f32[2,64,512]{2,1,0:T(8,128)S(1)}, f32[2,64,512]{2,1,0:T(8,128)}, u32[]{:S(2)}) copy-start(f32[2,64,512]{2,1,0:T(8,128)} %data.1) | copy-start | bytes 786436
  4.0 23.5 %copy-start.1 = (s32[2,64,512]{2,1,0:T(8,128)S(1)}, s32[2,64,512]{2,1,0:T(8,128)}, u32[]{:S(2)}) copy-start(s32[2,64,512]{2,1,0:T(8,128)} %mask.1) | copy-start | bytes 786436
  4.1 23.5 %copy-start.2 = (bf16[64,64]{1,0:T(8,128)(2,1)S(1)}, bf16[64,64]{1,0:T(8,128)(2,1)}, u32[]{:S(2)}) copy-start(bf16[64,64]{1,0:T(8,128)(2,1)} %basis.1) | copy-start | bytes 24580
  4.1 2.9 %collective-permute-start = (bf16[4,128,512]{2,1,0:T(8,128)(2,1)S(1)}, bf16[4,128,512]{2,1,0:T(8,128)(2,1)S(1)}, u32[]{:S(2)}, u32[]{:S(2)}) collective-permute-start(bf16[4,128,512]{2,1,0:T(8,128)(2,1)S(1)} %project.1), channel_id=1, source_target_pairs={{0,4},{4,0},{1,5},{5,1},{2,6},{6,2},{3,7},{7,3},{8,12},{12,8},{9,1... | collective-permute-start | bytes 1572872 | tf_op jit(solution)/shard_map/ppermute | solution.py:192
  41.6 7.8 %collective-permute-start.1 = (bf16[16,32,512]{2,1,0:T(8,128)(2,1)S(1)}, bf16[16,32,512]{2,1,0:T(8,128)(2,1)S(1)}, u32[]{:S(2)}, u32[]{:S(2)}) collective-permute-start(bf16[16,32,512]{2,1,0:T(8,128)(2,1)S(1)} %all_to_all.11.grad), channel_id=1, source_target_pairs={{0,4},{4,0},{1,5},{5,1},{2,6},{6,2},{3,7},{7,3},{8,12},{12,8},{9,1... | collective-permute-start | bytes 1572872 | tf_op jit(solution)/shard_map/ppermute | solution.py:192
where the time goes:
time: 51.6 us; the launch traced here: 51.4 us
  blocking collectives  33.5 us (65%)
  Pallas kernels  10.3 us (20%)
  starting transfers between devices  5.95 us (12%)
  other arithmetic  0.88 us (2%)
  between operations  0.71 us (1%)
    all_to_all x2, blocking collectives, exchange(): lax.all_to_all(x, axes, split_axis=0, concat_axis=0, tiled=True, axis_ind...  33.5 us
    ppermute x2, starting transfers between devices, swap(): return lax.ppermute(x, 'core', [(0, 1), (1, 0)])  5.95 us
    pallas_call x2, Pallas kernels, project(): pl.pallas_call(functools.partial(project_kernel, own), out_shape=[sums, w...  5.46 us
    pallas_call x2, Pallas kernels, spread(): pl.pallas_call(functools.partial(spread_kernel, own), out_shape=shape(lay...  3.9 us
  transfers between devices with their start and end apart: 2, of which 0 were waited for; matrix products, arithmetic and copies ran while one was open for 0% of the time, Pallas kernels for 9%

commit v1 on v0

--- a/solution.py
+++ b/solution.py
@@ -9,7 +9,6 @@
 
 F32, BF16 = jnp.float32, jnp.bfloat16
 MIB = 1024 * 1024
-NEAR = 2
 PARAMS = pltpu.CompilerParams(vmem_limit_bytes=44 * MIB)
 WIDE = pltpu.CompilerParams(vmem_limit_bytes=50 * MIB)
 
@@ -65,21 +64,21 @@
     return jnp.concatenate(pieces, axis=1)
 
 
-def turns(chips):
-    return [f * NEAR + n for n in range(NEAR) for f in reversed(range(chips // NEAR))]
+def turn(step, core, chips):
+    first = chips // 2 - 1 - step // 2 if step % 2 == 0 else chips // 2 + step // 2
+    return first + core * (chips - 1 - 2 * first)
 
 
 def project_kernel(own, numbers, volume, out, *refs):
-    offsets, small, tables, slab, sems = refs[-5:]
+    offsets, small, tables, slab, sems, sums = refs[-6:]
     layers, chips, _, m, width = volume.shape
     half = width // 2
-    order = turns(chips)
     core = lax.axis_index("core")
     which = core if own else 1 - core
 
     def fetch(layer, step):
         return pltpu.make_async_copy(
-            volume.at[layer, order[step], which], slab.at[layer, step], sems.at[layer, step]
+            volume.at[layer, turn(step, which, chips), which], slab.at[layer, step], sems.at[layer, step]
         )
 
     brought = pltpu.make_async_copy(numbers, offsets, small)
@@ -91,17 +90,28 @@
     fill_forward(tables, offsets)
     if own:
         fill_back(refs[0], offsets)
-    for layer in range(layers):
+    early = layers // 2
+
+    def product(side, members):
+        low, high = window(side, half)
+        rows = [slab[layer].reshape(chips * m, width)[:, low:high] for layer in members]
+        weights = tables[side, members[0] : members[-1] + 1]
+        return jnp.dot(
+            jnp.concatenate(rows, axis=1),
+            weights.reshape(len(members) * (high - low), half),
+            preferred_element_type=F32,
+        )
+
+    for layer in range(early):
         for step in range(chips):
             fetch(layer, step).wait()
     for side in range(2):
-        low, high = window(side, half)
-        rows = [slab[layer].reshape(chips * m, width)[:, low:high] for layer in range(layers)]
-        total = jnp.dot(
-            jnp.concatenate(rows, axis=1),
-            tables[side].reshape(layers * (high - low), half),
-            preferred_element_type=F32,
-        ).astype(out.dtype)
+        sums[side] = product(side, range(early))
+    for layer in range(early, layers):
+        for step in range(chips):
+            fetch(layer, step).wait()
+    for side in range(2):
+        total = (sums[side] + product(side, range(early, layers))).astype(out.dtype)
         out[:, :, side * half : (side + 1) * half] = total.reshape(chips, m, half)
 
 
@@ -155,11 +165,10 @@
 
     def store(layer, step):
         return pltpu.make_async_copy(
-            staged.at[layer, step], out.at[layer, order[step], which], sems.at[layer, step]
+            staged.at[layer, step], out.at[layer, turn(step, which, chips), which], sems.at[layer, step]
         )
 
     coef = grad.shape[0] // chips
-    order = turns(chips)
     joined = [grad[c * chips + step] for step in range(chips) for c in range(coef)]
     joined = jnp.concatenate(joined, axis=0)
     for layer in range(layers):
@@ -192,7 +201,11 @@
         return lax.ppermute(x, "core", [(0, 1), (1, 0)])
 
     groups = [
-        [(chip * 2 + core) * coef + c for c in range(coef) for chip in turns(chips)]
+        [
+            (turn(step, core, chips) * 2 + core) * coef + c
+            for c in range(coef)
+            for step in range(chips)
+        ]
         for core in range(2)
     ]
 
@@ -218,6 +231,7 @@
                 pltpu.VMEM((2, layers, half + half // 2, half), BF16),
                 pltpu.VMEM((layers, chips, m, width), BF16),
                 pltpu.SemaphoreType.DMA((layers, chips)),
+                pltpu.VMEM((2, chips * m, half), F32),
             ],
             compiler_params=WIDE,
             name="project" + ("_own" if own else ""),

time: 51.6 us -> 50.8 us (0.984)
  starting transfers between devices: 5.95 us -> 5.38 us
    ppermute x2, starting transfers between devices: 5.95 us -> 5.38 us  [swap(): return lax.ppermute(x, 'core', [(0, 1), (1, 0)])]
where the time goes in v1:
time: 50.8 us; the launch traced here: 50.6 us
  blocking collectives  33.6 us (66%)
  Pallas kernels  9.95 us (20%)
  starting transfers between devices  5.38 us (11%)
  other arithmetic  0.88 us (2%)
  between operations  0.71 us (1%)
    all_to_all x2, blocking collectives, exchange(): lax.all_to_all(x, axes, split_axis=0, concat_axis=0, tiled=True, axis_ind...  33.6 us
    ppermute x2, starting transfers between devices, swap(): return lax.ppermute(x, 'core', [(0, 1), (1, 0)])  5.38 us
    pallas_call x2, Pallas kernels, project(): pl.pallas_call(functools.partial(project_kernel, own), out_shape=[sums, w...  5.13 us
    pallas_call x2, Pallas kernels, spread(): pl.pallas_call(functools.partial(spread_kernel, own), out_shape=shape(lay...  3.9 us
  transfers between devices with their start and end apart: 2, of which 0 were waited for; matrix products, arithmetic and copies ran while one was open for 0% of the time, Pallas kernels for 9%

profile of v1, /device:TPU:1, one launch (start us, length us, event | category | flops | bytes accessed | tf_op | source)
XLA Modules:
  0.0 50.6 jit_solution(3725244524997496546)
XLA Ops:
  0.6 0.7 %multiply_add_fusion.numbers = s32[4]{0:T(128)S(1)} fusion(s32[4]{0:T(128)} %param.8, s32[4]{0:T(128)} %param.7), kind=kLoop, calls=%fused_computation.1 | loop fusion | flops 8 | bytes 48 | tf_op jit(solution)/shard_map/add | solution.py:218
  1.3 2.5 %project.1 = bf16[4,128,512]{2,1,0:T(8,128)(2,1)S(1)} custom-call(s32[4]{0:T(128)S(1)} %multiply_add_fusion.numbers, bf16[4,4,2,128,512]{4,3,2,1,0:T(8,128)(2,1)} %bitcast.6), custom_call_target="tpu_custom_call" | custom-call | tf_op jit(solution)/shard_map/project/pallas_call | solution.py:223
  3.8 0.0 copy-start
  3.8 0.0 copy-start.1
  3.9 0.0 copy-start.2
  3.9 0.1 collective-permute-start
  4.0 2.6 %project_own.1 = (f32[4,128,512]{2,1,0:T(8,128)S(1)}, bf16[2,4,256,256]{3,2,1,0:T(8,128)(2,1)S(1)}) custom-call(s32[4]{0:T(128)S(1)} %multiply_add_fusion.numbers, bf16[4,4,2,128,512]{4,3,2,1,0:T(8,128)(2,1)} %bitcast.7), custom_call_target="tpu_custom_call" | custom-call | tf_op jit(solution)/shard_map/project_own/pallas_call | solution.py:223
  6.6 0.0 collective-permute-done
  6.6 0.2 add_convert_fusion
  6.9 20.1 %all_to_all.10.sums_of = bf16[16,32,512]{2,1,0:T(8,128)(2,1)S(1)} all-to-all(bf16[16,32,512]{2,1,0:T(8,128)(2,1)S(1)} %bitcast.9), channel_id=1, replica_groups={{8,16,0,24,9,17,1,25,10,18,2,26,11,19,3,27},{20,12,28,4,21,13,29,5,22,1..., dimensions={0} | all-to-all | bytes 1048576 | tf_op jit(solution)/shard_map/all_to_all | solution.py:214
  27.0 0.0 copy-done
  27.0 0.0 copy-done.1
  27.0 0.0 copy-done.2
  27.0 0.9 %misfit.1 = (bf16[2,64,512]{2,1,0:T(8,128)(2,1)}, bf16[16,32,512]{2,1,0:T(8,128)(2,1)S(1)}) custom-call(bf16[64,64]{1,0:T(8,128)(2,1)S(1)} %copy-done.2, f32[2,64,512]{2,1,0:T(8,128)S(1)} %copy-done, s32[2,64,512]{2,1,0:T(8,128)S(1)} %copy-done.1, bf16[16,32,512]{2,1,0:T(8,128)(2,1)S(1)} %all_to_all.10.sums_of), custom_call_target="tpu_custom_call" | custom-call | tf_op jit(solution)/shard_map/misfit/pallas_call | solution.py:245
  27.9 13.5 %all_to_all.11.grad = bf16[16,32,512]{2,1,0:T(8,128)(2,1)S(1)} all-to-all(bf16[16,32,512]{2,1,0:T(8,128)(2,1)S(1)} %get-tuple-element.8), channel_id=1, replica_groups={{8,16,0,24,9,17,1,25,10,18,2,26,11,19,3,27},{20,12,28,4,21,13,29,5,22,1..., dimensions={0} | all-to-all | bytes 1048576 | tf_op jit(solution)/shard_map/all_to_all | solution.py:214
  41.4 5.3 %collective-permute-start.1 = (bf16[16,32,512]{2,1,0:T(8,128)(2,1)S(1)}, bf16[16,32,512]{2,1,0:T(8,128)(2,1)S(1)}, u32[]{:S(2)}, u32[]{:S(2)}) collective-permute-start(bf16[16,32,512]{2,1,0:T(8,128)(2,1)S(1)} %all_to_all.11.grad), channel_id=1, source_target_pairs={{0,4},{4,0},{1,5},{5,1},{2,6},{6,2},{3,7},{7,3},{8,12},{12,8},{9,1... | collective-permute-start | bytes 1572872 | tf_op jit(solution)/shard_map/ppermute | solution.py:201
  46.7 1.9 %spread_own.1.refs_0_ = bf16[4,4,2,128,512]{4,3,2,1,0:T(8,128)(2,1)} custom-call(bf16[2,4,256,256]{3,2,1,0:T(8,128)(2,1)S(1)} %get-tuple-element.6.tables, bf16[16,32,512]{2,1,0:T(8,128)(2,1)S(1)} %all_to_all.11.grad), custom_call_target="tpu_custom_call" | custom-call | tf_op jit(solution)/shard_map/spread_own/pallas_call | solution.py:257
  48.6 0.0 collective-permute-done.1.grad
  48.6 2.0 %spread.1 = bf16[4,4,2,128,512]{4,3,2,1,0:T(8,128)(2,1)} custom-call(bf16[2,4,256,256]{3,2,1,0:T(8,128)(2,1)S(1)} %get-tuple-element.6.tables, bf16[16,32,512]{2,1,0:T(8,128)(2,1)S(1)} %collective-permute-done.1.grad, bf16[4,4,2,128,512]{4,3,2,1,0:T(8,128)(2,1)} %spread_own.1.refs_0_), custom_call_target="tpu_custom_call", output_to_operand_aliasing={{}: (2, {})} | custom-call | tf_op jit(solution)/shard_map/spread/pallas_call | solution.py:257
  (1 shorter events, 0.0 us)
Async XLA Ops:
  3.8 23.2 %copy-start = (f32[2,64,512]{2,1,0:T(8,128)S(1)}, f32[2,64,512]{2,1,0:T(8,128)}, u32[]{:S(2)}) copy-start(f32[2,64,512]{2,1,0:T(8,128)} %data.1) | copy-start | bytes 786436
  3.8 23.2 %copy-start.1 = (s32[2,64,512]{2,1,0:T(8,128)S(1)}, s32[2,64,512]{2,1,0:T(8,128)}, u32[]{:S(2)}) copy-start(s32[2,64,512]{2,1,0:T(8,128)} %mask.1) | copy-start | bytes 786436
  3.9 23.2 %copy-start.2 = (bf16[64,64]{1,0:T(8,128)(2,1)S(1)}, bf16[64,64]{1,0:T(8,128)(2,1)}, u32[]{:S(2)}) copy-start(bf16[64,64]{1,0:T(8,128)(2,1)} %basis.1) | copy-start | bytes 24580
  3.9 2.7 %collective-permute-start = (bf16[4,128,512]{2,1,0:T(8,128)(2,1)S(1)}, bf16[4,128,512]{2,1,0:T(8,128)(2,1)S(1)}, u32[]{:S(2)}, u32[]{:S(2)}) collective-permute-start(bf16[4,128,512]{2,1,0:T(8,128)(2,1)S(1)} %project.1), channel_id=1, source_target_pairs={{0,4},{4,0},{1,5},{5,1},{2,6},{6,2},{3,7},{7,3},{8,12},{12,8},{9,1... | collective-permute-start | bytes 1572872 | tf_op jit(solution)/shard_map/ppermute | solution.py:201
  41.4 7.2 %collective-permute-start.1 = (bf16[16,32,512]{2,1,0:T(8,128)(2,1)S(1)}, bf16[16,32,512]{2,1,0:T(8,128)(2,1)S(1)}, u32[]{:S(2)}, u32[]{:S(2)}) collective-permute-start(bf16[16,32,512]{2,1,0:T(8,128)(2,1)S(1)} %all_to_all.11.grad), channel_id=1, source_target_pairs={{0,4},{4,0},{1,5},{5,1},{2,6},{6,2},{3,7},{7,3},{8,12},{12,8},{9,1... | collective-permute-start | bytes 1572872 | tf_op jit(solution)/shard_map/ppermute | solution.py:201

commit v2 on v1

--- a/solution.py
+++ b/solution.py
@@ -25,12 +25,18 @@
 
 def fill_forward(tables, offsets):
     _, layers, span, half = tables.shape
-    for side in range(2):
-        low, _ = window(side, half)
-        row = lax.broadcasted_iota(jnp.int32, (span, half), 0) + low
-        column = lax.broadcasted_iota(jnp.int32, (span, half), 1) + side * half
-        for layer in range(layers):
-            tables[side, layer] = weigh(column - row, offsets[layer])
+    quarter = half // 2
+    row = lax.broadcasted_iota(jnp.int32, (half, half), 0)
+    column = lax.broadcasted_iota(jnp.int32, (half, half), 1)
+    none = jnp.zeros((quarter, quarter), BF16)
+    for layer in range(layers):
+        weights = weigh(column - row, offsets[layer])
+        tables[0, layer, :half] = weights
+        tables[0, layer, half:, :quarter] = none
+        tables[0, layer, half:, quarter:] = weights[quarter:, :quarter]
+        tables[1, layer, :quarter, :quarter] = weights[:quarter, quarter:]
+        tables[1, layer, :quarter, quarter:] = none
+        tables[1, layer, quarter:] = weights
 
 
 def fill_back(tables, offsets):

time: 50.8 us -> 50.6 us (level)
  no operation moved by 1% of the time
where the time goes in v2:
time: 50.6 us; the launch traced here: 50.4 us
  blocking collectives  33.6 us (66%)
  Pallas kernels  9.79 us (19%)
  starting transfers between devices  5.38 us (11%)
  other arithmetic  0.88 us (2%)
  between operations  0.71 us (1%)
    all_to_all x2, blocking collectives, exchange(): lax.all_to_all(x, axes, split_axis=0, concat_axis=0, tiled=True, axis_ind...  33.6 us
    ppermute x2, starting transfers between devices, swap(): return lax.ppermute(x, 'core', [(0, 1), (1, 0)])  5.38 us
    pallas_call x2, Pallas kernels, project(): pl.pallas_call(functools.partial(project_kernel, own), out_shape=[sums, w...  4.97 us
    pallas_call x2, Pallas kernels, spread(): pl.pallas_call(functools.partial(spread_kernel, own), out_shape=shape(lay...  3.9 us
  transfers between devices with their start and end apart: 2, of which 0 were waited for; matrix products, arithmetic and copies ran while one was open for 0% of the time, Pallas kernels for 9%

profile of v2, /device:TPU:1, one launch (start us, length us, event | category | flops | bytes accessed | tf_op | source)
XLA Modules:
  0.0 50.4 jit_solution(3500401091522666576)
XLA Ops:
  0.6 0.7 %multiply_add_fusion.numbers = s32[4]{0:T(128)S(1)} fusion(s32[4]{0:T(128)} %param.8, s32[4]{0:T(128)} %param.7), kind=kLoop, calls=%fused_computation.1 | loop fusion | flops 8 | bytes 48 | tf_op jit(solution)/shard_map/add | solution.py:224
  1.3 2.5 %project.1 = bf16[4,128,512]{2,1,0:T(8,128)(2,1)S(1)} custom-call(s32[4]{0:T(128)S(1)} %multiply_add_fusion.numbers, bf16[4,4,2,128,512]{4,3,2,1,0:T(8,128)(2,1)} %bitcast.6), custom_call_target="tpu_custom_call" | custom-call | tf_op jit(solution)/shard_map/project/pallas_call | solution.py:229
  3.8 0.0 copy-start
  3.8 0.0 copy-start.1
  3.8 0.0 copy-start.2
  3.8 0.1 collective-permute-start
  3.9 2.5 %project_own.1 = (f32[4,128,512]{2,1,0:T(8,128)S(1)}, bf16[2,4,256,256]{3,2,1,0:T(8,128)(2,1)S(1)}) custom-call(s32[4]{0:T(128)S(1)} %multiply_add_fusion.numbers, bf16[4,4,2,128,512]{4,3,2,1,0:T(8,128)(2,1)} %bitcast.7), custom_call_target="tpu_custom_call" | custom-call | tf_op jit(solution)/shard_map/project_own/pallas_call | solution.py:229
  6.4 0.0 collective-permute-done
  6.5 0.2 add_convert_fusion
  6.7 20.1 %all_to_all.10.sums_of = bf16[16,32,512]{2,1,0:T(8,128)(2,1)S(1)} all-to-all(bf16[16,32,512]{2,1,0:T(8,128)(2,1)S(1)} %bitcast.9), channel_id=1, replica_groups={{8,16,0,24,9,17,1,25,10,18,2,26,11,19,3,27},{20,12,28,4,21,13,29,5,22,1..., dimensions={0} | all-to-all | bytes 1048576 | tf_op jit(solution)/shard_map/all_to_all | solution.py:220
  26.8 0.0 copy-done
  26.8 0.0 copy-done.1
  26.8 0.0 copy-done.2
  26.8 0.9 %misfit.1 = (bf16[2,64,512]{2,1,0:T(8,128)(2,1)}, bf16[16,32,512]{2,1,0:T(8,128)(2,1)S(1)}) custom-call(bf16[64,64]{1,0:T(8,128)(2,1)S(1)} %copy-done.2, f32[2,64,512]{2,1,0:T(8,128)S(1)} %copy-done, s32[2,64,512]{2,1,0:T(8,128)S(1)} %copy-done.1, bf16[16,32,512]{2,1,0:T(8,128)(2,1)S(1)} %all_to_all.10.sums_of), custom_call_target="tpu_custom_call" | custom-call | tf_op jit(solution)/shard_map/misfit/pallas_call | solution.py:251
  27.7 13.5 %all_to_all.11.grad = bf16[16,32,512]{2,1,0:T(8,128)(2,1)S(1)} all-to-all(bf16[16,32,512]{2,1,0:T(8,128)(2,1)S(1)} %get-tuple-element.8), channel_id=1, replica_groups={{8,16,0,24,9,17,1,25,10,18,2,26,11,19,3,27},{20,12,28,4,21,13,29,5,22,1..., dimensions={0} | all-to-all | bytes 1048576 | tf_op jit(solution)/shard_map/all_to_all | solution.py:220
  41.2 5.3 %collective-permute-start.1 = (bf16[16,32,512]{2,1,0:T(8,128)(2,1)S(1)}, bf16[16,32,512]{2,1,0:T(8,128)(2,1)S(1)}, u32[]{:S(2)}, u32[]{:S(2)}) collective-permute-start(bf16[16,32,512]{2,1,0:T(8,128)(2,1)S(1)} %all_to_all.11.grad), channel_id=1, source_target_pairs={{0,4},{4,0},{1,5},{5,1},{2,6},{6,2},{3,7},{7,3},{8,12},{12,8},{9,1... | collective-permute-start | bytes 1572872 | tf_op jit(solution)/shard_map/ppermute | solution.py:207
  46.5 1.9 %spread_own.1.refs_0_ = bf16[4,4,2,128,512]{4,3,2,1,0:T(8,128)(2,1)} custom-call(bf16[2,4,256,256]{3,2,1,0:T(8,128)(2,1)S(1)} %get-tuple-element.6.tables, bf16[16,32,512]{2,1,0:T(8,128)(2,1)S(1)} %all_to_all.11.grad), custom_call_target="tpu_custom_call" | custom-call | tf_op jit(solution)/shard_map/spread_own/pallas_call | solution.py:263
  48.4 0.0 collective-permute-done.1.grad
  48.4 2.0 %spread.1 = bf16[4,4,2,128,512]{4,3,2,1,0:T(8,128)(2,1)} custom-call(bf16[2,4,256,256]{3,2,1,0:T(8,128)(2,1)S(1)} %get-tuple-element.6.tables, bf16[16,32,512]{2,1,0:T(8,128)(2,1)S(1)} %collective-permute-done.1.grad, bf16[4,4,2,128,512]{4,3,2,1,0:T(8,128)(2,1)} %spread_own.1.refs_0_), custom_call_target="tpu_custom_call", output_to_operand_aliasing={{}: (2, {})} | custom-call | tf_op jit(solution)/shard_map/spread/pallas_call | solution.py:263
  (1 shorter events, 0.0 us)
Async XLA Ops:
  3.8 23.0 %copy-start = (f32[2,64,512]{2,1,0:T(8,128)S(1)}, f32[2,64,512]{2,1,0:T(8,128)}, u32[]{:S(2)}) copy-start(f32[2,64,512]{2,1,0:T(8,128)} %data.1) | copy-start | bytes 786436
  3.8 23.0 %copy-start.1 = (s32[2,64,512]{2,1,0:T(8,128)S(1)}, s32[2,64,512]{2,1,0:T(8,128)}, u32[]{:S(2)}) copy-start(s32[2,64,512]{2,1,0:T(8,128)} %mask.1) | copy-start | bytes 786436
  3.8 23.0 %copy-start.2 = (bf16[64,64]{1,0:T(8,128)(2,1)S(1)}, bf16[64,64]{1,0:T(8,128)(2,1)}, u32[]{:S(2)}) copy-start(bf16[64,64]{1,0:T(8,128)(2,1)} %basis.1) | copy-start | bytes 24580
  3.8 2.6 %collective-permute-start = (bf16[4,128,512]{2,1,0:T(8,128)(2,1)S(1)}, bf16[4,128,512]{2,1,0:T(8,128)(2,1)S(1)}, u32[]{:S(2)}, u32[]{:S(2)}) collective-permute-start(bf16[4,128,512]{2,1,0:T(8,128)(2,1)S(1)} %project.1), channel_id=1, source_target_pairs={{0,4},{4,0},{1,5},{5,1},{2,6},{6,2},{3,7},{7,3},{8,12},{12,8},{9,1... | collective-permute-start | bytes 1572872 | tf_op jit(solution)/shard_map/ppermute | solution.py:207
  41.2 7.2 %collective-permute-start.1 = (bf16[16,32,512]{2,1,0:T(8,128)(2,1)S(1)}, bf16[16,32,512]{2,1,0:T(8,128)(2,1)S(1)}, u32[]{:S(2)}, u32[]{:S(2)}) collective-permute-start(bf16[16,32,512]{2,1,0:T(8,128)(2,1)S(1)} %all_to_all.11.grad), channel_id=1, source_target_pairs={{0,4},{4,0},{1,5},{5,1},{2,6},{6,2},{3,7},{7,3},{8,12},{12,8},{9,1... | collective-permute-start | bytes 1572872 | tf_op jit(solution)/shard_map/ppermute | solution.py:207

commit v3 on v2

--- a/solution.py
+++ b/solution.py
@@ -96,7 +96,7 @@
     fill_forward(tables, offsets)
     if own:
         fill_back(refs[0], offsets)
-    early = layers // 2
+    early = layers - layers // 4
 
     def product(side, members):
         low, high = window(side, half)

time: 50.6 us -> 51.2 us (1.012)
  Pallas kernels: 9.79 us -> 10.4 us
    pallas_call x2, Pallas kernels: 4.97 us -> 5.53 us  [project(): pl.pallas_call(functools.partial(project_kernel, own), out_shape=[sums, w...]
where the time goes in v3:
time: 51.2 us; the launch traced here: 50.9 us
  blocking collectives  33.6 us (66%)
  Pallas kernels  10.4 us (20%)
  starting transfers between devices  5.38 us (11%)
  other arithmetic  0.88 us (2%)
  between operations  0.71 us (1%)
    all_to_all x2, blocking collectives, exchange(): lax.all_to_all(x, axes, split_axis=0, concat_axis=0, tiled=True, axis_ind...  33.6 us
    pallas_call x2, Pallas kernels, project(): pl.pallas_call(functools.partial(project_kernel, own), out_shape=[sums, w...  5.53 us
    ppermute x2, starting transfers between devices, swap(): return lax.ppermute(x, 'core', [(0, 1), (1, 0)])  5.38 us
    pallas_call x2, Pallas kernels, spread(): pl.pallas_call(functools.partial(spread_kernel, own), out_shape=shape(lay...  3.9 us
  transfers between devices with their start and end apart: 2, of which 0 were waited for; matrix products, arithmetic and copies ran while one was open for 0% of the time, Pallas kernels for 9%

profile of v3, /device:TPU:1, one launch (start us, length us, event | category | flops | bytes accessed | tf_op | source)
XLA Modules:
  0.0 50.9 jit_solution(17606166694536878241)
XLA Ops:
  0.6 0.7 %multiply_add_fusion.numbers = s32[4]{0:T(128)S(1)} fusion(s32[4]{0:T(128)} %param.8, s32[4]{0:T(128)} %param.7), kind=kLoop, calls=%fused_computation.1 | loop fusion | flops 8 | bytes 48 | tf_op jit(solution)/shard_map/add | solution.py:224
  1.3 2.8 %project.1 = bf16[4,128,512]{2,1,0:T(8,128)(2,1)S(1)} custom-call(s32[4]{0:T(128)S(1)} %multiply_add_fusion.numbers, bf16[4,4,2,128,512]{4,3,2,1,0:T(8,128)(2,1)} %bitcast.6), custom_call_target="tpu_custom_call" | custom-call | tf_op jit(solution)/shard_map/project/pallas_call | solution.py:229
  4.1 0.0 copy-start
  4.1 0.0 copy-start.1
  4.1 0.0 copy-start.2
  4.1 0.1 collective-permute-start
  4.2 2.8 %project_own.1 = (f32[4,128,512]{2,1,0:T(8,128)S(1)}, bf16[2,4,256,256]{3,2,1,0:T(8,128)(2,1)S(1)}) custom-call(s32[4]{0:T(128)S(1)} %multiply_add_fusion.numbers, bf16[4,4,2,128,512]{4,3,2,1,0:T(8,128)(2,1)} %bitcast.7), custom_call_target="tpu_custom_call" | custom-call | tf_op jit(solution)/shard_map/project_own/pallas_call | solution.py:229
  7.0 0.0 collective-permute-done
  7.0 0.2 add_convert_fusion
  7.3 20.1 %all_to_all.10.sums_of = bf16[16,32,512]{2,1,0:T(8,128)(2,1)S(1)} all-to-all(bf16[16,32,512]{2,1,0:T(8,128)(2,1)S(1)} %bitcast.9), channel_id=1, replica_groups={{8,16,0,24,9,17,1,25,10,18,2,26,11,19,3,27},{20,12,28,4,21,13,29,5,22,1..., dimensions={0} | all-to-all | bytes 1048576 | tf_op jit(solution)/shard_map/all_to_all | solution.py:220
  27.4 0.0 copy-done
  27.4 0.0 copy-done.1
  27.4 0.0 copy-done.2
  27.4 0.9 %misfit.1 = (bf16[2,64,512]{2,1,0:T(8,128)(2,1)}, bf16[16,32,512]{2,1,0:T(8,128)(2,1)S(1)}) custom-call(bf16[64,64]{1,0:T(8,128)(2,1)S(1)} %copy-done.2, f32[2,64,512]{2,1,0:T(8,128)S(1)} %copy-done, s32[2,64,512]{2,1,0:T(8,128)S(1)} %copy-done.1, bf16[16,32,512]{2,1,0:T(8,128)(2,1)S(1)} %all_to_all.10.sums_of), custom_call_target="tpu_custom_call" | custom-call | tf_op jit(solution)/shard_map/misfit/pallas_call | solution.py:251
  28.3 13.5 %all_to_all.11.grad = bf16[16,32,512]{2,1,0:T(8,128)(2,1)S(1)} all-to-all(bf16[16,32,512]{2,1,0:T(8,128)(2,1)S(1)} %get-tuple-element.8), channel_id=1, replica_groups={{8,16,0,24,9,17,1,25,10,18,2,26,11,19,3,27},{20,12,28,4,21,13,29,5,22,1..., dimensions={0} | all-to-all | bytes 1048576 | tf_op jit(solution)/shard_map/all_to_all | solution.py:220
  41.8 5.3 %collective-permute-start.1 = (bf16[16,32,512]{2,1,0:T(8,128)(2,1)S(1)}, bf16[16,32,512]{2,1,0:T(8,128)(2,1)S(1)}, u32[]{:S(2)}, u32[]{:S(2)}) collective-permute-start(bf16[16,32,512]{2,1,0:T(8,128)(2,1)S(1)} %all_to_all.11.grad), channel_id=1, source_target_pairs={{0,4},{4,0},{1,5},{5,1},{2,6},{6,2},{3,7},{7,3},{8,12},{12,8},{9,1... | collective-permute-start | bytes 1572872 | tf_op jit(solution)/shard_map/ppermute | solution.py:207
  47.0 1.9 %spread_own.1.refs_0_ = bf16[4,4,2,128,512]{4,3,2,1,0:T(8,128)(2,1)} custom-call(bf16[2,4,256,256]{3,2,1,0:T(8,128)(2,1)S(1)} %get-tuple-element.6.tables, bf16[16,32,512]{2,1,0:T(8,128)(2,1)S(1)} %all_to_all.11.grad), custom_call_target="tpu_custom_call" | custom-call | tf_op jit(solution)/shard_map/spread_own/pallas_call | solution.py:263
  49.0 0.0 collective-permute-done.1.grad
  49.0 2.0 %spread.1 = bf16[4,4,2,128,512]{4,3,2,1,0:T(8,128)(2,1)} custom-call(bf16[2,4,256,256]{3,2,1,0:T(8,128)(2,1)S(1)} %get-tuple-element.6.tables, bf16[16,32,512]{2,1,0:T(8,128)(2,1)S(1)} %collective-permute-done.1.grad, bf16[4,4,2,128,512]{4,3,2,1,0:T(8,128)(2,1)} %spread_own.1.refs_0_), custom_call_target="tpu_custom_call", output_to_operand_aliasing={{}: (2, {})} | custom-call | tf_op jit(solution)/shard_map/spread/pallas_call | solution.py:263
  (1 shorter events, 0.0 us)
Async XLA Ops:
  4.1 23.3 %copy-start = (f32[2,64,512]{2,1,0:T(8,128)S(1)}, f32[2,64,512]{2,1,0:T(8,128)}, u32[]{:S(2)}) copy-start(f32[2,64,512]{2,1,0:T(8,128)} %data.1) | copy-start | bytes 786436
  4.1 23.3 %copy-start.1 = (s32[2,64,512]{2,1,0:T(8,128)S(1)}, s32[2,64,512]{2,1,0:T(8,128)}, u32[]{:S(2)}) copy-start(s32[2,64,512]{2,1,0:T(8,128)} %mask.1) | copy-start | bytes 786436
  4.1 23.3 %copy-start.2 = (bf16[64,64]{1,0:T(8,128)(2,1)S(1)}, bf16[64,64]{1,0:T(8,128)(2,1)}, u32[]{:S(2)}) copy-start(bf16[64,64]{1,0:T(8,128)(2,1)} %basis.1) | copy-start | bytes 24580
  4.1 2.9 %collective-permute-start = (bf16[4,128,512]{2,1,0:T(8,128)(2,1)S(1)}, bf16[4,128,512]{2,1,0:T(8,128)(2,1)S(1)}, u32[]{:S(2)}, u32[]{:S(2)}) collective-permute-start(bf16[4,128,512]{2,1,0:T(8,128)(2,1)S(1)} %project.1), channel_id=1, source_target_pairs={{0,4},{4,0},{1,5},{5,1},{2,6},{6,2},{3,7},{7,3},{8,12},{12,8},{9,1... | collective-permute-start | bytes 1572872 | tf_op jit(solution)/shard_map/ppermute | solution.py:207
  41.8 7.2 %collective-permute-start.1 = (bf16[16,32,512]{2,1,0:T(8,128)(2,1)S(1)}, bf16[16,32,512]{2,1,0:T(8,128)(2,1)S(1)}, u32[]{:S(2)}, u32[]{:S(2)}) collective-permute-start(bf16[16,32,512]{2,1,0:T(8,128)(2,1)S(1)} %all_to_all.11.grad), channel_id=1, source_target_pairs={{0,4},{4,0},{1,5},{5,1},{2,6},{6,2},{3,7},{7,3},{8,12},{12,8},{9,1... | collective-permute-start | bytes 1572872 | tf_op jit(solution)/shard_map/ppermute | solution.py:207
